TPU v7x, 128 devices: a whole 4x4x4 slice. The times are simulated.
128 devices in a mesh: seq: 64 (over z, y, x), mp: 2 (over core).
Axes of the slice: x: 4, y: 4, z: 4, core: 2. Of those that a mesh axis runs over, the one named last changes fastest.
Arguments:
- tokens: bfloat16 [16384, 2048], P('seq'), may hold values from -6 to 6
- cotangent: bfloat16 [16384, 2048], P('seq'), may hold values from -6 to 6
- starts: int32 [16384], P('seq'), may hold values from 0 to 1, as said below
- valid: int32 [16384], P('seq'), may hold values 0 or 1
- w_rec: bfloat16 [2048, 2, 2560], P('seq', None, 'mp'), may hold values from -0.125 to 0.125
- w_out: bfloat16 [2560, 2048], P('mp', 'seq'), may hold values from -0.25 to 0.25
- w_mlp: bfloat16 [2048, 2, 6144], P('seq', None, 'mp'), may hold values from -0.125 to 0.125
- w_down: bfloat16 [6144, 2048], P('mp', 'seq'), may hold values from -0.15625 to 0.15625
- lru_gates: bfloat16 [2, 10, 256, 256], P(None, 'mp'), may hold values from -0.375 to 0.375
- lru_bias: float32 [2, 2560], P(None, 'mp'), may hold values from -4 to 4
- lam: float32 [2560], P('mp'), may hold values from 4 to 16
- conv_w: float32 [4, 2560], P(None, 'mp'), may hold values from -3 to 3
- conv_b: float32 [2560], P('mp'), may hold values from -2 to 2
- gain_rec: float32 [2048], replicated, may hold values from 0.1 to 1.9
- gain_mlp: float32 [2048], replicated, may hold values from 0.1 to 1.9
- h_init: float32 [2560], P('mp'), may hold values from -5 to 5
- conv_state: float32 [3, 2560], P(None, 'mp'), may hold values from -5 to 5
Outputs:
- result: bfloat16 [16384, 2048], P('seq')
- rms_rec: float32 [16384], P('seq')
- rms_mlp: float32 [16384], P('seq')
- grad_tokens: float32 [16384, 2048], P('seq')
- grad_w_rec: float32 [2048, 2, 2560], P('seq', None, 'mp')
- grad_w_out: float32 [2560, 2048], P('mp', 'seq')
- grad_w_mlp: float32 [2048, 2, 6144], P('seq', None, 'mp')
- grad_w_down: float32 [6144, 2048], P('mp', 'seq')
- grad_lru_gates: float32 [2, 10, 256, 256], P(None, 'mp')
- grad_lru_bias: float32 [2, 2560], P(None, 'mp')
- grad_lam: float32 [2560], P('mp')
- grad_conv_w: float32 [4, 2560], P(None, 'mp')
- conv_bias_gradient: float32 [2560], P('mp')
- grad_gain_rec: float32 [2048], replicated
- grad_gain_mlp: float32 [2048], replicated
- grad_h_init: float32 [2560], P('mp')
- grad_conv_state: float32 [3, 2560], P(None, 'mp')
Inputs may be any that keep to these rules, and one draw needn't show every extreme that they name: `starts`: 1 at exactly two tokens: one among the first 256 tokens but not the very first, one among the last 256; 0 elsewhere.
All inputs are finite; a program needn't handle non-finite values. No bound on the sum of `valid` on one device may be relied on, other than what follows from the above.
Results may differ from a plain program's by a relative error of at most 0.018.
Values may be sent and summed in bfloat16 or wider, within the bound.
A program may use at most 448 MiB of HBM per device.

v0:
```python
import functools
import jax
import jax.numpy as jnp
from jax import lax
from jax.experimental import pallas as pl
from jax.experimental.pallas import tpu as pltpu
from jax.sharding import Mesh, PartitionSpec as P

CONV = 4
EDGE = CONV - 1
BLOCK = 256
EPSILON = 1e-06
MESH = pl.DeviceIdType.MESH
ANY = pl.BlockSpec(memory_space=pl.ANY)
HBM = pl.BlockSpec(memory_space=pltpu.HBM)
VM = pl.BlockSpec(memory_space=pltpu.VMEM)
MIB = 1024 * 1024
AXES = ("z", "y", "x")
SEQ = ("z", "y", "x")
ORDERS = (("x", "y", "z"), ("y", "z", "x"), ("z", "x", "y"))
F32, BF16 = jnp.float32, jnp.bfloat16
GELU_C, GELU_A = 0.7978845608028654, 0.044715
DMA = pltpu.SemaphoreType.DMA


def loop(lower, upper, step, batch):
    main = lower + (upper - lower) // batch * batch

    def several(k, carry):
        for i in range(batch):
            step(lower + k * batch + i, 0)
        return carry

    if main > lower:
        lax.fori_loop(0, (main - lower) // batch, several, 0)
    for i in range(main, upper):
        step(i, 0)


def dot(left, right):
    return jnp.dot(left, right, preferred_element_type=F32)


def dot_t(left, right):
    return lax.dot_general(left, right, (((1,), (1,)), ((), ())), preferred_element_type=F32)


def outer(left, right):
    return lax.dot_general(left, right, (((0,), (0,)), ((), ())), preferred_element_type=F32)


def greet(peers):
    sem = pltpu.get_barrier_semaphore()
    for peer in peers:
        pl.semaphore_signal(sem, inc=1, device_id=peer, device_id_type=MESH)
    pl.semaphore_wait(sem, len(peers))


def push(src, dst, send, recv, peer):
    return pltpu.make_async_remote_copy(
        src_ref=src, dst_ref=dst, send_sem=send, recv_sem=recv, device_id=peer, device_id_type=MESH
    )


def ring(axis):
    me = lax.axis_index(axis)
    return me, lax.rem(me + 1, 4), lax.rem(me + 2, 4), lax.rem(me + 3, 4)


def all_neighbours():
    peers = []
    for axis in AXES:
        _, up, _, down = ring(axis)
        peers += [{axis: up}, {axis: down}]
    return peers


def params(cid, mib):
    return pltpu.CompilerParams(
        collective_id=cid, has_side_effects=True, vmem_limit_bytes=mib * MIB
    )


def part_of(done, axis, index, rows, cols):
    spot = []
    for name in AXES:
        if name in done:
            spot.append(pl.ds(0, 4))
        elif name == axis:
            spot.append(index)
        else:
            spot.append(lax.axis_index(name))
    return tuple(spot) + (rows, cols)


def pick(names, axis, index, others):
    spot, rest = [], iter(others)
    for name in names:
        spot.append(index if name == axis else next(rest))
    return tuple(spot)


class Scatter:
    def __init__(self, entry, src, cols, order, halves, bufs, out, own_sem, send, recv, band=None, rings=1):
        self.rings = 0 if halves is None else rings
        self.band, self.band_rows = band, src.shape[-2] if band is None else band[1]
        self.entry, self.src, self.order = entry, src, order
        self.start, self.width = cols
        self.halves, self.bufs, self.out = halves, list(bufs), out
        self.own_sem, self.send, self.recv = own_sem, send, recv
        self.left, self.sent = AXES, []

    def view(self, at, rows=None):
        if rows is None:
            first = self.band[0] if self.band is not None and self.phase == 0 else 0
            rows = pl.ds(first, self.band_rows)
        return at + (rows, pl.ds(self.start if self.phase == 0 else 0, self.width))

    def spread(self, i):
        return ((i // 4, lax.rem(i, 4)), (i,), ())[self.phase]

    def copy(self, src, dst, way, kind, peer):
        at = (self.entry, self.phase, way, kind)
        copy = push(src, dst, self.send.at[at], self.recv.at[at], {self.axis: peer})
        copy.start()
        self.sent.append(copy)
        return copy

    def load(self, index, dst, rows=None):
        src = self.src.at[self.view(pick(self.left, self.axis, index, self.full), rows)]
        copy = pltpu.make_async_copy(src, dst, self.own_sem.at[self.entry, len(self.loads)])
        copy.start()
        self.loads.append(copy)

    def begin(self, phase):
        self.phase, self.axis = phase, self.order[phase]
        self.full = (pl.ds(0, 4),) * (2 - phase)
        me, up, far, down = ring(self.axis)
        self.first, self.second, self.loads = [], [], []
        self.two_step = phase < self.rings
        if self.two_step:
            self.ones, self.twos = self.bufs.pop(0), self.bufs.pop(0)
            self.near = self.bufs.pop(0) if phase == 0 else None
            for way, peer in enumerate((up, down)):
                half = self.halves[way]
                src = self.src.at[self.view(pick(self.left, self.axis, far, self.full), half)]
                self.first.append(self.copy(src, self.ones.at[way], way, 0, peer))
            for way, peer in enumerate((up, down)):
                half = self.halves[1 - way]
                src = self.src.at[self.view(pick(self.left, self.axis, peer, self.full), half)]
                dst = self.twos.at[(way,) + self.full + (half,)]
                self.second.append(self.copy(src, dst, way, 1, peer))
            for way, peer in enumerate((up, down)):
                if phase == 0:
                    self.load(peer, self.near.at[way], self.halves[way])
        else:
            self.threes = self.bufs.pop(0)
            for step, peer in enumerate((up, far, down)):
                src = self.src.at[self.view(pick(self.left, self.axis, peer, self.full))]
                self.second.append(self.copy(src, self.threes.at[step], step, 0, peer))
        if phase == 0:
            self.own = self.bufs.pop(0)
            self.load(me, self.own)
        self.acc = self.bufs.pop(0) if phase < 2 else self.out

    def middle(self):
        _, up, _, down = ring(self.axis)
        for way, peer in enumerate((up, down)):
            self.first[way].wait_recv()
            if self.phase == 0:
                self.loads[way].wait()

            def add(i, carry, way=way, peer=peer):
                there = (way,) + self.spread(i)
                if self.phase == 0:
                    own = self.near[there]
                else:
                    at = pick(self.left, self.axis, peer, self.spread(i))
                    own = self.src[self.view(at, self.halves[way])]
                total = self.ones[there].astype(F32) + own.astype(F32)
                self.ones[there] = total.astype(BF16)
                return carry

            lax.fori_loop(0, 4 ** (2 - self.phase), add, 0)
            dst = self.twos.at[(way,) + self.full + (self.halves[way],)]
            self.second.append(self.copy(self.ones.at[way], dst, way, 2, peer))

    def finish(self):
        me = lax.axis_index(self.axis)
        for copy in self.second:
            copy.wait_recv()
        if self.phase == 0:
            self.loads[-1].wait()
        buf, slots = (self.twos, (0, 1)) if self.two_step else (self.threes, (0, 1, 2))

        def total(i, carry):
            there = self.spread(i)
            if self.phase == 0:
                whole = self.own[there].astype(F32)
            else:
                whole = self.src[self.view(pick(self.left, self.axis, me, there))].astype(F32)
            for slot in slots:
                whole = whole + buf[(slot,) + there].astype(F32)
            if self.phase < 2:
                self.acc[there] = whole.astype(self.acc.dtype)
            else:
                first = 0 if self.band is None else self.band[0]
                self.acc[pl.ds(first, self.band_rows), pl.ds(self.start, self.width)] = whole
            return carry

        lax.fori_loop(0, 4 ** (2 - self.phase), total, 0)
        self.src = self.acc
        self.left = tuple(name for name in self.left if name != self.axis)

    def drain(self):
        for copy in self.sent:
            copy.wait_send()


def scatter_buffers(rows, width, rings):
    bufs = []
    for phase in range(3):
        cube = (4,) * (2 - phase)
        if phase < rings:
            bufs.append(pltpu.VMEM((2,) + cube + (rows // 2, width), BF16))
            bufs.append(pltpu.VMEM((2,) + cube + (rows, width), BF16))
            if phase == 0:
                bufs.append(pltpu.VMEM((2,) + cube + (rows // 2, width), BF16))
        else:
            bufs.append(pltpu.VMEM((3,) + cube + (rows, width), BF16))
        if phase == 0:
            bufs.append(pltpu.VMEM(cube + (rows, width), BF16))
        if phase < 2:
            bufs.append(pltpu.VMEM(cube + (rows, width), BF16))
    return bufs


class Gather:
    def __init__(self, entry, out, order, cols, send, recv, done=(), ring_rounds=(), band=None):
        self.band = (0, out.shape[3]) if band is None else band
        self.entry, self.out, self.order, self.cols = entry, out, order, pl.ds(*cols)
        self.send, self.recv, self.sent = send, recv, []
        self.done, self.ring_rounds = done, ring_rounds

    def spot(self, origin, rows=None):
        rows = pl.ds(*self.band) if rows is None else rows
        return self.out.at[part_of(self.done, self.axis, origin, rows, self.cols)]

    def copy(self, src, dst, step, way, peer):
        at = (self.entry, self.phase, step, way)
        copy = push(src, dst, self.send.at[at], self.recv.at[at], {self.axis: peer})
        copy.start()
        self.sent.append(copy)
        return copy

    def begin(self, phase, src=None):
        self.phase, self.axis = phase, self.order[phase]
        me, up, far, down = ring(self.axis)
        here = self.spot(me)
        src = here if src is None else src.at[:, self.cols]
        peers = (up, down) if phase in self.ring_rounds else (up, far, down)
        self.copies = [self.copy(src, here, 0, way, peer) for way, peer in enumerate(peers)]

    def middle(self):
        _, up, _, down = ring(self.axis)
        half = self.out.shape[3] // 2
        first, self.copies = self.copies, []
        for way, (peer, origin) in enumerate(((up, down), (down, up))):
            first[way].wait_recv()
            spot = self.spot(origin, pl.ds(way * half, half))
            self.copies.append(self.copy(spot, spot, 1, way, peer))

    def hold(self):
        for copy in self.copies:
            copy.wait_recv()

    def finish(self):
        self.hold()
        self.done = self.done + (self.axis,)

    def drain(self):
        for copy in self.sent:
            copy.wait_send()


class Rounds:
    def __init__(self, slots, send, recv, entry=0, order=("x", "y", "z")):
        self.slots, self.send, self.recv, self.sent = slots, send, recv, []
        self.entry, self.order = entry, order

    def begin(self, phase, rows):
        self.phase, axis = phase, self.order[phase]
        me = lax.axis_index(axis)
        for at, value in rows:
            self.slots[phase, me, at] = value
        self.copies = []
        for step, peer in enumerate(ring(axis)[1:]):
            spot = self.slots.at[phase, me]
            at = (self.entry, phase, step)
            copy = push(spot, spot, self.send.at[at], self.recv.at[at], {axis: peer})
            copy.start()
            self.copies.append(copy)

    def finish(self):
        for copy in self.copies:
            copy.wait_recv()
        self.sent += self.copies

    def drain(self):
        for copy in self.sent:
            copy.wait_send()


class Prefix(Rounds):
    def start(self, pair, backward):
        self.backward, self.cur, self.head = backward, pair, None
        self.share(0)

    def share(self, phase):
        self.begin(phase, [(slice(0, 1), self.cur[0]), (slice(1, 2), self.cur[1])])

    def step(self):
        self.finish()
        me = lax.axis_index(self.order[self.phase])
        run = (jnp.ones_like(self.cur[0]), jnp.zeros_like(self.cur[1]))
        mine = run
        for j in (3, 2, 1, 0) if self.backward else (0, 1, 2, 3):
            take = me == j
            mine = (jnp.where(take, run[0], mine[0]), jnp.where(take, run[1], mine[1]))
            fac, val = self.slots[self.phase, j, 0:1], self.slots[self.phase, j, 1:2]
            run = (run[0] * fac, val + fac * run[1])
        self.cur = run
        if self.head is None:
            self.head = mine
        else:
            self.head = (mine[0] * self.head[0], self.head[1] + self.head[0] * mine[1])
        if self.phase < 2:
            self.share(self.phase + 1)
        return self.head


class Total(Rounds):
    def start(self, value):
        self.begin(0, [(slice(None), value)])

    def step(self):
        self.finish()
        at = self.slots
        k = self.phase
        value = (at[k, 0] + at[k, 1]) + (at[k, 2] + at[k, 3])
        if k + 1 < len(self.order):
            self.begin(k + 1, [(slice(None), value)])
        return value


def axis_peers():
    return [{axis: ring(axis)[step]} for axis in AXES for step in (1, 2, 3)]


def along_seq(distance):
    place = lax.axis_index("z") * 16 + lax.axis_index("y") * 4 + lax.axis_index("x")
    place = lax.rem(place + distance + 64, 64)
    return {"z": place // 16, "y": lax.rem(place // 4, 4), "x": lax.rem(place, 4)}


CHUNKS = ((0, 384), (384, 512), (896, 384))
SUM_ORDERS = (
    (("y", "z", "x"), ("x", "y", "z"), ("z", "y", "x")),
    (("z", "x", "y"), ("x", "z", "y"), ("y", "x", "z")),
    (("y", "z", "x"), ("x", "y", "z"), ("z", "x", "y")),
)
ROW_HALVES = (pl.ds(0, 16), pl.ds(16, 16))
BANDS = ((0, 16), (16, 16), (32, 16))


def gelu_parts(x):
    inner = GELU_C * (x + GELU_A * x * x * x)
    t = jnp.tanh(inner)
    slope = GELU_C * (1.0 + 3.0 * GELU_A * x * x)
    return 0.5 * x * (1.0 + t), 0.5 * (1.0 + t) + 0.5 * x * (1.0 - t * t) * slope


FAR, UP, DOWN, ME = 0, 1, 2, 3


class RingSum:
    def __init__(self, part, got, one, two, send, recv, sib_send, sib_recv):
        self.part, self.got, self.one, self.two = part, got, one, two
        self.send, self.recv, self.sib_send, self.sib_recv = send, recv, sib_send, sib_recv
        self.core, self.sums, self.sent = lax.axis_index("mp"), {}, []

    def across(self, *slots):
        for slot in slots:
            copy = push(
                self.part.at[slot, 1 - self.core],
                self.got.at[slot],
                self.sib_send.at[slot],
                self.sib_recv.at[slot],
                {"mp": 1 - self.core},
            )
            copy.start()
            self.sums[slot] = copy

    def add(self, dst, src):
        dst[...] = (dst[...].astype(F32) + src[...].astype(F32)).astype(dst.dtype)

    def collect(self, slot):
        self.sums[slot].wait_recv()
        self.add(self.got.at[slot], self.part.at[slot, self.core])

    def far(self):
        self.collect(FAR)
        half = self.one.shape[1]
        _, up, _, down = ring("x")
        self.first = []
        for way, peer in enumerate((up, down)):
            piece = self.got.at[FAR, pl.ds(way * half, half)]
            at = (0, way)
            copy = push(piece, self.one.at[way], self.send.at[at], self.recv.at[at], {"x": peer})
            copy.start()
            self.first.append(copy)

    def near(self):
        half = self.one.shape[1]
        _, up, _, down = ring("x")
        self.second = []
        for way, (peer, slot) in enumerate(((up, UP), (down, DOWN))):
            self.collect(slot)
            self.first[way].wait_recv()
            self.add(self.got.at[slot, pl.ds(way * half, half)], self.one.at[way])
            at = (1, way)
            copy = push(self.got.at[slot], self.two.at[way], self.send.at[at], self.recv.at[at], {"x": peer})
            copy.start()
            self.second.append(copy)

    def total(self):
        self.sums[ME].wait_recv()
        total = self.got[ME].astype(F32) + self.part[ME, self.core].astype(F32)
        for way in range(2):
            self.second[way].wait_recv()
            total = total + self.two[way].astype(F32)
        return total

    def drain(self):
        for copy in self.first + self.second + list(self.sums.values()):
            copy.wait_send()


def ring_sum_scratch(rows, width):
    return [
        pltpu.VMEM((4, rows, width), BF16),
        pltpu.VMEM((2, rows // 2, width), BF16),
        pltpu.VMEM((2, rows, width), BF16),
        DMA((2, 2)),
        DMA((2, 2)),
        DMA((4,)),
        DMA((4,)),
    ]


def mlp_kernel(
    nm_ref, go_ref, hidden_ref, inv_ref, gain_ref, go_hbm, w_hbm,
    grad_hidden_ref, low_ref, term_ref, dw_ref, opart_out,
    go, w, gathered, npart, opart, mlp_in, ggu, gmi, low_half,
    load_sem, wsend, wrecv, gsend, grecv, gsib_send, gsib_recv, core_sem, *sum_refs,
):
    rows, width = nm_ref.shape
    half = rows // 2
    units = mlp_in.shape[1]
    me, up, far, down = ring("x")
    core = lax.axis_index("mp")
    other = {"mp": 1 - core}
    loads = [pltpu.make_async_copy(nm_ref, gathered.at[ME, core], load_sem.at[0])]
    wide = w.shape[4] // 2
    full, every = pl.ds(0, 4), pl.ds(0, w.shape[3])
    last = (("z", 0), ("y", wide))

    def weight_set(axis, index, at, cols):
        return ((index, full) if axis == "z" else (full, index)) + (full, at, pl.ds(cols, wide))

    for e, (axis, cols) in enumerate(last):
        here, ahead, _, behind = ring(axis)
        for k, index in enumerate((here, ahead, behind)):
            spot = weight_set(axis, index, every, cols)
            loads.append(pltpu.make_async_copy(w_hbm.at[spot], w.at[spot], load_sem.at[1 + 3 * e + k]))
    for slot, chip in ((FAR, far), (UP, up), (DOWN, down), (ME, me)):
        at = pl.ds(slot * 2 * rows, 2 * rows)
        loads.append(pltpu.make_async_copy(go_hbm.at[chip], go.at[at], load_sem.at[7 + slot]))
    for load in loads:
        load.start()
    peers = [{"x": up}, {"x": down}, other]
    for axis in ("y", "z"):
        peers += [{axis: ring(axis)[1]}, {axis: ring(axis)[3]}]
    greet(peers)
    top, low = pl.ds(0, half), pl.ds(half, half)
    first = []
    for way, (peer, slot) in enumerate(((up, DOWN), (down, UP))):
        spot = gathered.at[slot, core]
        copy = push(nm_ref, spot, gsend.at[0, way], grecv.at[0, way], {"x": peer})
        copy.start()
        first.append(copy)
    across = [push(nm_ref, gathered.at[ME, core], gsib_send.at[0], gsib_recv.at[0], other)]
    across[0].start()
    rest = []
    for e, (axis, cols) in enumerate(last):
        _, ahead, _, behind = ring(axis)
        deep = w.shape[3] // 2
        for way, (peer, origin) in enumerate(((ahead, behind), (behind, ahead))):
            spot = weight_set(axis, origin, pl.ds(way * deep, deep), cols)
            copy = push(w_hbm.at[spot], w.at[spot], wsend.at[e, way], wrecv.at[e, way], {axis: peer})
            copy.start()
            rest.append(copy)
    second = []
    for way, (peer, slot, piece) in enumerate(((up, DOWN, top), (down, UP, low))):
        first[way].wait_recv()
        spot = gathered.at[slot, core]
        copy = push(
            spot.at[piece], gathered.at[FAR, core, piece], gsend.at[1, way], grecv.at[1, way], {"x": peer}
        )
        copy.start()
        second.append(copy)
        copy = push(spot, spot, gsib_send.at[1 + way], gsib_recv.at[1 + way], other)
        copy.start()
        across.append(copy)
    for copy in rest:
        copy.wait_recv()
    for load in loads:
        load.wait()

    def tile(j, start=0):
        return pl.ds(pl.multiple_of(start + j * 256, 256), 256)

    def columns(at):
        return w[:, :, :, :, at].reshape(width, 256)

    def shard_tile(i, at):
        return w[i // 2, pl.ds(2 * lax.rem(i, 2), 2), :, :, at].reshape(256, -1)

    def grad_tile(j, carry):
        gmi[:, tile(j)] = dot(go[...], columns(tile(j, 2 * units)))
        return carry

    loop(0, units // 256, grad_tile, 1)
    for way, piece in enumerate((top, low)):
        second[way].wait_recv()
        spot = gathered.at[FAR, core, piece]
        copy = push(spot, spot, gsib_send.at[3 + way], gsib_recv.at[3 + way], other)
        copy.start()
        across.append(copy)

    def tokens_step(slot):
        at = pl.ds(slot * 2 * rows, 4 * rows)

        def hidden_tile(j, carry):
            tokens_in = gathered[slot : slot + 2].reshape(4 * rows, width)
            gate = dot(tokens_in, columns(tile(j)))
            up_lin = dot(tokens_in, columns(tile(j, units)))
            grad = gmi[at, tile(j)]
            act, slope = gelu_parts(gate)
            mlp_in[at, tile(j)] = (act * up_lin).astype(BF16)
            ggu[at, tile(j)] = (slope * (grad * up_lin)).astype(BF16)
            ggu[at, tile(j, units)] = (grad * act).astype(BF16)
            return carry

        loop(0, units // 256, hidden_tile, 1)

        def back_tile(j, carry):
            back = dot_t(ggu[at], shard_tile(j, pl.ds(0, 2 * units)))
            npart[slot : slot + 2, :, :, tile(j)] = back.astype(BF16).reshape(2, 2, rows, 256)
            return carry

        loop(0, width // 256, back_tile, 1)

    def out_tile(j, carry):
        part = dot_t(mlp_in[...], shard_tile(j, pl.ds(2 * units, units)))
        opart[:, :, :, tile(j)] = part.astype(BF16).reshape(4, 2, rows, 256)
        return carry

    def weight_grads(lower, upper):
        def step(i, carry):
            left = gathered[:, :, :, tile(i)].reshape(8 * rows, 256)
            dw_ref[tile(i), pl.ds(0, 2 * units)] = outer(left, ggu[...]).astype(BF16)
            dw_ref[tile(i), pl.ds(2 * units, units)] = outer(go[:, tile(i)], mlp_in[...]).astype(BF16)
            return carry

        loop(lower, upper, step, 1)

    sums = RingSum(npart, *sum_refs)
    for copy in across:
        copy.wait_recv()
    tokens_step(FAR)
    sums.across(FAR, UP)
    sums.far()
    tokens_step(DOWN)
    sums.across(DOWN, ME)
    sums.near()
    loop(0, width // 256, out_tile, 1)
    save = pltpu.make_async_copy(opart, opart_out, load_sem.at[11])
    save.start()
    weight_grads(0, 5)
    grad_normed = sums.total()
    hat = hidden_ref[...] * inv_ref[...]
    grad_hat = grad_normed * gain_ref[...]
    inner = jnp.mean(grad_hat * hat, axis=-1, keepdims=True)
    grad_hidden = go_ref[...].astype(F32) + inv_ref[...] * (grad_hat - hat * inner)
    grad_hidden_ref[...] = grad_hidden
    term_ref[...] = jnp.sum(grad_normed * hat, axis=0, keepdims=True)
    low_half[...] = grad_hidden.astype(BF16)
    low_ref[core] = low_half[...]
    swap = push(low_half, low_ref.at[core], core_sem.at[0], core_sem.at[1], other)
    swap.start()
    weight_grads(5, 8)
    swap.wait()
    save.wait()
    sums.drain()
    for copy in first + second + across + rest:
        copy.wait_send()


def mlp(normed, grad_out, hidden, inverse, gain, grad_out_all, weights, cid):
    rows, width = normed.shape
    units = weights.shape[4] // 3

    def block(dtype, *shape):
        return pltpu.VMEM(shape, dtype)

    return pl.pallas_call(
        mlp_kernel,
        out_shape=[
            jax.ShapeDtypeStruct((rows, width), F32),
            jax.ShapeDtypeStruct((2, rows, width), BF16),
            jax.ShapeDtypeStruct((1, width), F32),
            jax.ShapeDtypeStruct((width, 3 * units), BF16),
            jax.ShapeDtypeStruct((4, 2, rows, width), BF16),
        ],
        in_specs=[VM] * 5 + [ANY] * 2,
        out_specs=[VM] * 4 + [HBM],
        scratch_shapes=[
            block(BF16, 8 * rows, width),
            block(BF16, *weights.shape),
            block(BF16, 4, 2, rows, width),
            block(BF16, 4, 2, rows, width),
            block(BF16, 4, 2, rows, width),
            block(BF16, 8 * rows, units),
            block(BF16, 8 * rows, 2 * units),
            block(F32, 8 * rows, units),
            block(BF16, rows, width),
        ]
        + [DMA((12,)), DMA((2, 2)), DMA((2, 2)), DMA((2, 2)), DMA((2, 2)), DMA((5,)), DMA((5,)), DMA((2,))]
        + ring_sum_scratch(rows, width),
        compiler_params=params(cid, 60),
    )(normed, grad_out, hidden, inverse, gain, grad_out_all.reshape(4, 2 * rows, width), weights)


def lanes(n):
    return pl.ds(pl.multiple_of(n * BLOCK, BLOCK), BLOCK)


def minus_expm1(x):
    series = jnp.ones_like(x)
    for k in (9, 8, 7, 6, 5, 4, 3, 2):
        series = 1.0 + x * (1.0 / k) * series
    return jnp.where(x > -0.4, -x * series, 1.0 - jnp.exp(x))


def log1p(x):
    series = jnp.zeros_like(x)
    for k in (7, 6, 5, 4, 3, 2, 1):
        series = 1.0 / k - x * series
    return jnp.where(x < 0.05, x * series, jnp.log(1.0 + x))


CONV_W, CONV_B, RATES, BIAS, CONV_STATE, H_INIT, SLOPE = 0, 4, 5, 6, 8, 11, 12


def rec_forward_kernel(*refs):
    (
        tokens_ref, gain_ref, gain_mlp_ref, conv_w_ref, conv_b_ref, lam_ref, bias_ref, conv_state_ref,
        h_init_ref, starts_ref, valid_ref, rec_raw, back_in, mlp_raw, down_in, cot_ref, g_hbm,
        lin_out, gate_out, back_out, mlp_out, ext_out, act_out, mixed_out, reset_out, input_out, f_out, states_out,
        branch_out, normed_out, go_all, inv_ref, rms_ref, hidden_ref, nm_ref, inv_mlp_ref, rms_mlp_ref, go_ref, v_ref,
        wl, wg, wb, ext, gate_lin, mixed_v, reset_v, input_v, f_v, states, branch_v, normed, tail_in, driven, cf_v,
        part, part_low, part_in, g_v, rms_v, slots, mask_ref, rec_in, mlp_in,
        tail_sem, load_sem, save_sem, own_sem, move_send, move_recv, send, recv, small_send, small_recv, core_sem,
        go_send, go_recv, go_sib_send, go_sib_recv,
    ) = refs
    count, width = tokens_ref.shape
    rec = f_v.shape[1]
    for k in range(2):
        rec_in[:, k * rec : (k + 1) * rec] = rec_raw[:, k, :]
        mlp_in[:, k * mlp_raw.shape[2] : (k + 1) * mlp_raw.shape[2]] = mlp_raw[:, k, :]
    gate_in, lin_in = rec_in.at[:, pl.ds(0, rec)], rec_in.at[:, pl.ds(rec, rec)]
    blocks = rec // BLOCK
    half = count // 2
    core = lax.axis_index("mp")
    other = {"mp": 1 - core}
    here = tuple(lax.axis_index(name) for name in AXES)
    load = pltpu.make_async_copy(g_hbm, g_v, load_sem)
    load.start()
    owns = [
        pltpu.make_async_copy(lin_in, wl.at[here], own_sem.at[0]),
        pltpu.make_async_copy(gate_in, wg.at[here], own_sem.at[1]),
        pltpu.make_async_copy(back_in, wb.at[here], own_sem.at[2]),
    ]
    units = mlp_out.shape[4] // 3
    every = pl.ds(0, rec_in.shape[0])

    def quarter(k, chip):
        if k == 2:
            return down_in.at[every, pl.ds(pl.multiple_of(chip * units, units), units)]
        return mlp_in.at[every, pl.ds(pl.multiple_of((4 * k + chip) * units, units), units)]

    spots = [mlp_out.at[here + (every, pl.ds(k * units, units))] for k in range(3)]
    owns += [pltpu.make_async_copy(quarter(k, here[2]), spots[k], own_sem.at[3 + k]) for k in range(3)]
    for own in owns:
        own.start()
    greet(axis_peers() + [other, along_seq(1), along_seq(-1)])
    tail_copy = push(tokens_ref.at[pl.ds(count - 16, 16)], tail_in, tail_sem.at[0], tail_sem.at[1], along_seq(1))
    tail_copy.start()
    lin = [Gather(e, wl, ORDERS[e], CHUNKS[e], send, recv, ring_rounds=(2,)) for e in range(3)]
    gate = [
        Gather(3 + e, wg, ORDERS[(e + 1) % 3], CHUNKS[e], send, recv, ring_rounds=(1, 2)) for e in range(3)
    ]
    back = [
        Gather(6 + e, wb, ORDERS[(2, 1, 0)[e]], CHUNKS[e], send, recv, ring_rounds=(1, 2)) for e in range(3)
    ]
    rest = gate + back
    wide = mlp_out.shape[4] // 2
    mlp_flows = [
        Gather(9 + e, mlp_out, order, (e * wide, wide), send, recv, done=("x",), ring_rounds=(1,))
        for e, order in enumerate((("y", "z"), ("z", "y")))
    ]

    def each(group, name, *args):
        for flow in group:
            getattr(flow, name)(*args)

    each(lin, "begin", 0, lin_in)
    moves = []
    for step, peer in enumerate(ring("x")[1:]):
        for k in range(3):
            copy = push(quarter(k, peer), spots[k], move_send.at[step, k], move_recv.at[step, k], {"x": peer})
            copy.start()
            moves.append(copy)
    each(gate, "begin", 0, gate_in)
    each(back, "begin", 0, back_in)

    v_ref[CONV_W : CONV_W + CONV] = conv_w_ref[...]
    v_ref[BIAS : BIAS + 2] = bias_ref[...]
    v_ref[CONV_STATE : CONV_STATE + EDGE] = conv_state_ref[...]
    for at, ref in ((CONV_B, conv_b_ref), (H_INIT, h_init_ref)):
        v_ref[at : at + 1] = ref[...].reshape(1, rec)
    lam = lam_ref[...].reshape(1, rec)
    v_ref[RATES : RATES + 1] = jnp.maximum(-lam, 0.0) + log1p(jnp.exp(-jnp.abs(lam)))
    v_ref[SLOPE : SLOPE + 1] = 1.0 / (1.0 + jnp.exp(lam))
    v_ref[SLOPE + 1 :] = jnp.zeros((15 - SLOPE, rec), F32)
    square = (count, count)
    diagonal = lax.broadcasted_iota(jnp.int32, square, 0) == lax.broadcasted_iota(jnp.int32, square, 1)
    for k, row in enumerate((1.0 - starts_ref[...].astype(F32), valid_ref[...].astype(F32))):
        spread = jnp.where(diagonal, jnp.broadcast_to(row.reshape(1, count), square), 0.0)
        mask_ref[:, k : k + 1] = jnp.sum(spread, axis=1, keepdims=True)

    def norm(values):
        mean_sq = jnp.mean(values * values, axis=-1, keepdims=True)
        inverse = lax.rsqrt(mean_sq + EPSILON)
        return values * inverse, inverse, jnp.sqrt(mean_sq + EPSILON)

    def norm_step(i, carry):
        at = pl.ds(pl.multiple_of(i * 64, 64), 64)
        hat, inverse, rms = norm(tokens_ref[at].astype(F32))
        inv_ref[at] = inverse
        rms_ref[at] = rms
        normed[pl.ds(pl.multiple_of(16 + i * 64, 16), 64)] = (hat * gain_ref[...]).astype(BF16)
        return carry

    lax.fori_loop(0, count // 64, norm_step, 0)
    for own in owns:
        own.wait()
    each(lin, "finish")
    each(lin, "begin", 1)
    each(rest, "finish")
    each(rest, "begin", 1)
    tail_copy.wait_recv()
    normed[0:16] = (norm(tail_in[...].astype(F32))[0] * gain_ref[...]).astype(BF16)
    saves = []

    def save(src, dst):
        copy = pltpu.make_async_copy(src, dst, save_sem.at[len(saves)])
        copy.start()
        saves.append(copy)

    save(normed.at[pl.ds(16, count)], normed_out)
    each(lin, "finish")
    each(lin, "begin", 2)
    for copy in moves:
        copy.wait_recv()
    each(mlp_flows, "begin", 0)
    each(rest, "middle")
    each(lin, "middle")
    each(rest, "finish")
    each(rest, "begin", 2)
    mine = pl.ds(pl.multiple_of(core * half, half), half)
    go_ref[...] = (cot_ref[mine].astype(F32) * mask_ref[mine, 1:2]).astype(BF16)
    load.wait()
    each(lin, "finish")
    save(wl, lin_out)
    is_first = (here[0] + here[1] + here[2]) == 0

    def rec_step(n, carry):
        at = lanes(n)
        ext[:, at] = dot(normed[...], wl[:, :, :, :, at].reshape(width, BLOCK))

        @pl.when(is_first)
        def _():
            ext[16 - EDGE : 16, at] = v_ref[CONV_STATE : CONV_STATE + EDGE, at]

        total = v_ref[CONV_B : CONV_B + 1, at] + jnp.zeros((count, BLOCK), F32)
        for k in range(CONV):
            total = total + v_ref[CONV_W + k : CONV_W + k + 1, at] * ext[pl.ds(16 - EDGE + k, count), at]
        mixed = total.astype(BF16)
        mixed_v[:, at] = mixed
        reset = jax.nn.sigmoid(dot(mixed, g_v[0, n]) + v_ref[BIAS : BIAS + 1, at])
        gated = jax.nn.sigmoid(dot(mixed, g_v[1, n]) + v_ref[BIAS + 1 : BIAS + 2, at])
        reset_v[:, at] = reset
        input_v[:, at] = gated
        log_decay = -8.0 * v_ref[RATES : RATES + 1, at] * reset
        f_v[:, at] = jnp.exp(log_decay) * mask_ref[:, 0:1]
        driven[:, at] = jnp.sqrt(minus_expm1(2.0 * log_decay)) * gated * mixed.astype(F32)
        return carry

    lax.fori_loop(0, blocks, rec_step, 0)
    for src, dst in ((ext, ext_out), (mixed_v, mixed_out), (reset_v, reset_out), (input_v, input_out), (f_v, f_out)):
        save(src, dst)

    def group(i, carry):
        base = pl.multiple_of(i * 8, 8)
        f, d = f_v[pl.ds(base, 8)], driven[pl.ds(base, 8)]
        cf, cd = carry
        cfs, cds = [], []
        for r in range(8):
            cf = cf * f[r : r + 1]
            cd = cd * f[r : r + 1] + d[r : r + 1]
            cfs.append(cf)
            cds.append(cd)
        cf_v[pl.ds(base, 8)] = jnp.concatenate(cfs, axis=0)
        states[pl.ds(pl.multiple_of(base + 8, 8), 8)] = jnp.concatenate(cds, axis=0)
        return cf, cd

    zero = jnp.zeros((1, rec), F32)
    ends = lax.fori_loop(0, count // 8, group, (zero + 1.0, zero))
    prefix = Prefix(slots, small_send, small_recv)
    prefix.start(ends, False)
    by_axis = {axis: [flow for flow in rest if flow.axis == axis] for axis in AXES}
    each(by_axis["x"], "middle")
    prefix.step()
    each(by_axis["y"], "middle")
    each(mlp_flows, "finish")
    mlp_flows[1].begin(1)
    prefix.step()
    each(by_axis["z"], "middle")
    mlp_flows[0].begin(1)
    x_here, x_up, x_far, x_down = ring("x")
    spot = go_all.at[x_here, core]
    save(go_ref, spot)
    go_first = []
    for way, peer in enumerate((x_up, x_down)):
        copy = push(go_ref, spot, go_send.at[0, way], go_recv.at[0, way], {"x": peer})
        copy.start()
        go_first.append(copy)
    go_across = [push(go_ref, spot, go_sib_send.at[0], go_sib_recv.at[0], other)]
    go_across[0].start()
    head = prefix.step()
    carry_in = head[1] + head[0] * v_ref[H_INIT : H_INIT + 1]
    each(gate, "finish")
    save(wg, gate_out)

    def gate_step(n, carry):
        gate_lin[:, lanes(n)] = dot(normed[16:], wg[:, :, :, :, lanes(n)].reshape(width, BLOCK))
        return carry

    lax.fori_loop(0, blocks, gate_step, 0)
    save(gate_lin, act_out)
    states[0:8] = jnp.broadcast_to(carry_in, (8, rec))

    def branch_step(n, carry):
        at = lanes(n)
        value = states[8:, at] + cf_v[:, at] * states[0:1, at]
        states[8:, at] = value
        branch_v[:, at] = (gelu_parts(gate_lin[:, at])[0] * value).astype(BF16)
        return carry

    lax.fori_loop(0, blocks, branch_step, 0)
    save(states, states_out)
    save(branch_v, branch_out)
    each(back, "finish")
    save(wb, back_out)

    def out_step(i, carry):
        at = pl.ds(pl.multiple_of(i * 256, 256), 256)
        rows = wb[i // 2, pl.ds(2 * lax.rem(i, 2), 2)].reshape(256, rec)
        value = dot_t(branch_v[...], rows)
        part[0, :, at] = value[:half]
        part[1, :, at] = value[half:]
        return carry

    lax.fori_loop(0, width // 256, out_step, 0)
    part_low[...] = part[1 - core].astype(BF16)
    part_copy = push(part_low, part_in, core_sem.at[0], core_sem.at[1], other)
    part_copy.start()
    go_second = []
    for way, (peer, origin) in enumerate(((x_up, x_down), (x_down, x_up))):
        go_first[way].wait_recv()
        spot = go_all.at[origin, core]
        piece = spot.at[pl.ds(way * (half // 2), half // 2)]
        copy = push(piece, piece, go_send.at[1, way], go_recv.at[1, way], {"x": peer})
        copy.start()
        go_second.append(copy)
        copy = push(spot, spot, go_sib_send.at[1 + way], go_sib_recv.at[1 + way], other)
        copy.start()
        go_across.append(copy)
    part_copy.wait_recv()
    hidden = tokens_ref[mine].astype(F32) + (part[core] + part_in[...].astype(F32))
    hidden_ref[...] = hidden
    hat, inverse, rms = norm(hidden)
    inv_mlp_ref[...] = inverse
    rms_v[...] = jnp.broadcast_to(rms, (half, 128))
    rms_mlp_ref[core] = rms_v[...]
    rms_copy = push(rms_v, rms_mlp_ref.at[core], core_sem.at[2], core_sem.at[3], other)
    rms_copy.start()
    nm_ref[...] = (hat * gain_mlp_ref[...]).astype(BF16)
    for way in range(2):
        go_second[way].wait_recv()
        piece = go_all.at[x_far, core, pl.ds(way * (half // 2), half // 2)]
        copy = push(piece, piece, go_sib_send.at[3 + way], go_sib_recv.at[3 + way], other)
        copy.start()
        go_across.append(copy)
    each(mlp_flows, "hold")
    rms_copy.wait()
    for copy in go_across:
        copy.wait()
    for copy in go_first + go_second:
        copy.wait_send()
    for copy in moves:
        copy.wait_send()
    for copy in saves:
        copy.wait()
    each(lin, "drain")
    each(rest, "drain")
    each(mlp_flows, "drain")
    prefix.drain()
    part_copy.wait_send()
    tail_copy.wait_send()


def rec_forward(tokens, gain_rec, gain_mlp, vectors, masks, w_rec, back, w_mlp, down, cotangent, gates, cid):
    count, width = tokens.shape
    rows, rec = back.shape
    half = count // 2

    def cube(last):
        return (4, 4, 4, rows, last)

    def sds(shape, dtype):
        return jax.ShapeDtypeStruct(shape, dtype)

    saved = [
        (cube(rec), BF16),
        (cube(rec), BF16),
        (cube(rec), BF16),
        (cube(3 * down.shape[1] // 4), BF16),
        ((count + 16, rec), F32),
        ((count, rec), F32),
        ((count, rec), BF16),
        ((count, rec), F32),
        ((count, rec), F32),
        ((count, rec), F32),
        ((count + 8, rec), F32),
        ((count, rec), BF16),
        ((count, width), BF16),
        ((4, 2, half, width), BF16),
    ]
    small = [
        ((count, 1), F32),
        ((count, 1), F32),
        ((half, width), F32),
        ((half, width), BF16),
        ((half, 1), F32),
        ((2, half, 128), F32),
        ((half, width), BF16),
        ((16, rec), F32),
    ]
    scratch = saved[:3] + saved[4:12] + [((count + 16, width), BF16), ((16, width), BF16)]
    scratch += [((count, rec), F32), ((count, rec), F32), ((2, half, width), F32)]
    scratch += [((half, width), BF16), ((half, width), BF16), (gates.shape, BF16), ((half, 128), F32), ((3, 4, 2, rec), F32), ((count, 2), F32)]
    scratch += [((rows, 2 * rec), BF16), ((rows, 2 * w_mlp.shape[2]), BF16)]
    return pl.pallas_call(
        rec_forward_kernel,
        out_shape=[sds(*one) for one in saved + small],
        in_specs=[VM] * 16 + [ANY],
        out_specs=[HBM] * len(saved) + [VM] * len(small),
        scratch_shapes=[pltpu.VMEM(*one) for one in scratch]
        + [
            DMA((2,)),
            DMA,
            DMA((13,)),
            DMA((6,)),
            DMA((3, 3)),
            DMA((3, 3)),
            DMA((11, 3, 2, 3)),
            DMA((11, 3, 2, 3)),
            DMA((1, 3, 3)),
            DMA((1, 3, 3)),
            DMA((4,)),
            DMA((2, 2)),
            DMA((2, 2)),
            DMA((5,)),
            DMA((5,)),
        ],
        compiler_params=params(cid, 60),
    )(tokens, gain_rec[None], gain_mlp[None], *vectors, *masks, w_rec, back, w_mlp, down, cotangent, gates)


G_BIAS, G_LAM, G_CONV_W, G_CONV_B, G_H, G_STATE = 0, 2, 3, 7, 8, 9
GATE_ROWS = 48


def shard_rows(ref, i, value):
    value = value.reshape(2, 4, 32, value.shape[1])
    ref[i // 2, pl.ds(2 * lax.rem(i, 2), 2)] = value


def rec_back_kernel(
    gh_ref, branch_ref, normed_ref, gate_ref, states_ref, f_ref, v_ref, hidden_ref,
    wb_hbm, ext_hbm, mixed_hbm, reset_hbm, input_hbm, g_hbm, wg_hbm, opart_hbm,
    small_ref, part_ref, low, result_ref, dw_out_hbm, dw_gate_hbm, gg_hbm,
    wb, ext, mixed_v, reset_v, input_v, g_v, wg, opart, gate_low, cb, al, gm, dw_out, dw_gate, gg,
    tail, edge, edge_in, slots, result_half,
    *refs,
):
    load_sem, save_sem, small_send, small_recv, edge_sem, core_sem = refs[:6]
    sum_refs = refs[6:]
    count, rec = gate_ref.shape
    half = count // 2
    width = gh_ref.shape[1]
    blocks = rec // BLOCK
    pairs = (
        (wb_hbm, wb), (ext_hbm, ext), (mixed_hbm, mixed_v), (reset_hbm, reset_v), (input_hbm, input_v), (g_hbm, g_v),
        (wg_hbm, wg), (opart_hbm, opart),
    )
    loads = [pltpu.make_async_copy(src, dst, load_sem.at[k]) for k, (src, dst) in enumerate(pairs)]
    for load in loads:
        load.start()
    saves = []

    def save(src, dst):
        copy = pltpu.make_async_copy(src, dst, save_sem.at[len(saves)])
        copy.start()
        saves.append(copy)

    ahead, behind = along_seq(1), along_seq(-1)
    other = {"mp": 1 - lax.axis_index("mp")}
    greet(axis_peers() + [ahead, behind, other])
    place = lax.axis_index("z") * 16 + lax.axis_index("y") * 4 + lax.axis_index("x")
    is_first = jnp.where(place == 0, 1.0, 0.0)
    has_next = jnp.where(place == 63, 0.0, 1.0)

    def weight_grad(ref, left, right):
        def step(i, carry):
            cols = pl.ds(pl.multiple_of(i * 256, 256), 256)
            shard_rows(ref, i, outer(left[:, cols], right[...]).astype(BF16))
            return carry

        loop(0, left.shape[1] // 256, step, 1)

    loads[0].wait()

    def branch_step(n, carry):
        grad = dot(gh_ref[...], wb[:, lanes(n)])
        act, slope = gelu_parts(gate_ref[:, lanes(n)])
        gate_low[:, lanes(n)] = (slope * (grad * states_ref[8:, lanes(n)])).astype(BF16)
        al[:, lanes(n)] = grad * act
        return carry

    loop(0, blocks, branch_step, 1)
    loads[7].wait()
    sums = RingSum(opart, *sum_refs)
    sums.across(FAR, UP, DOWN, ME)

    def group(i, carry):
        base = pl.multiple_of(count - 8 - i * 8, 8)
        f, d = f_ref[pl.ds(base, 8)], al[pl.ds(base, 8)]
        follow, cf, cd = carry
        cfs, cds = [None] * 8, [None] * 8
        for r in (7, 6, 5, 4, 3, 2, 1, 0):
            cf = cf * follow
            cd = cd * follow + d[r : r + 1]
            cfs[r], cds[r] = cf, cd
            follow = f[r : r + 1]
        cb[pl.ds(base, 8)] = jnp.concatenate(cfs, axis=0)
        al[pl.ds(base, 8)] = jnp.concatenate(cds, axis=0)
        return follow, cf, cd

    zero = jnp.zeros((1, rec), F32)
    follow, cf, cd = lax.fori_loop(0, count // 8, group, (zero + 1.0, zero + 1.0, zero))
    prefix = Prefix(slots, small_send, small_recv)
    prefix.start((follow * cf, follow * cd), True)
    weight_grad(dw_out, gh_ref, branch_ref)
    save(dw_out, dw_out_hbm)
    prefix.step()
    sums.far()
    weight_grad(dw_gate, normed_ref, gate_low)
    save(dw_gate, dw_gate_hbm)
    prefix.step()
    for load in loads[1:7]:
        load.wait()

    def part_tile(i, carry):
        at = pl.ds(pl.multiple_of(i * 256, 256), 256)
        value = dot_t(gate_low[...], wg[at, :])
        part_ref[0, :, at] = value[:half]
        part_ref[1, :, at] = value[half:]
        return carry

    lax.fori_loop(0, width // 256, part_tile, 0)
    later = prefix.step()[1]
    sums.near()
    al[...] = al[...] + cb[...] * later

    def grads_step(n, carry):
        at = lanes(n)
        adjoint = al[:, at]
        factors, reset, gated = f_ref[:, at], reset_v[:, at], input_v[:, at]
        mixed_low = mixed_v[:, at]
        mixed = mixed_low.astype(F32)
        rates = v_ref[RATES : RATES + 1, at]
        log_decay = -8.0 * rates * reset
        decays = jnp.exp(log_decay)
        scale_in = jnp.sqrt(minus_expm1(2.0 * log_decay))
        grad_log = adjoint * states_ref[pl.ds(7, count), at] * factors
        grad_log = grad_log - adjoint * gated * mixed * decays * decays / scale_in
        small_ref[G_LAM : G_LAM + 1, at] = (
            8.0 * jnp.sum(grad_log * reset, axis=0, keepdims=True) * v_ref[SLOPE : SLOPE + 1, at]
        )
        small_ref[G_H : G_H + 1, at] = is_first * factors[0:1] * adjoint[0:1]
        grad_reset = (grad_log * (-8.0 * rates) * reset * (1.0 - reset)).astype(BF16)
        grad_input = (adjoint * scale_in * mixed * gated * (1.0 - gated)).astype(BF16)
        for g, grad in enumerate((grad_reset, grad_input)):
            small_ref[G_BIAS + g : G_BIAS + g + 1, at] = jnp.sum(
                grad.astype(F32), axis=0, keepdims=True
            )
            b = g * blocks + n
            rows = pl.ds(pl.multiple_of(16 * lax.rem(b, 3), 16), 16)
            gg[:, :, b // 3, rows, :] = outer(mixed_low, grad).astype(BF16).reshape(4, 4, 16, BLOCK)
        grad_mixed = adjoint * scale_in * gated
        grad_mixed = grad_mixed + dot_t(grad_reset, g_v[0, n]) + dot_t(grad_input, g_v[1, n])
        gm[0:8] = jnp.zeros((8, BLOCK), F32)
        gm[8 : 8 + count] = grad_mixed
        gm[8 + count :] = jnp.zeros((8, BLOCK), F32)
        small_ref[G_CONV_B : G_CONV_B + 1, at] = jnp.sum(grad_mixed, axis=0, keepdims=True)
        total = jnp.zeros((count, BLOCK), F32)
        front = jnp.zeros((8, BLOCK), F32)
        for k in range(CONV):
            small_ref[G_CONV_W + k : G_CONV_W + k + 1, at] = jnp.sum(
                grad_mixed * ext[pl.ds(16 - EDGE + k, count), at], axis=0, keepdims=True
            )
            weight = v_ref[CONV_W + k : CONV_W + k + 1, at]
            total = total + weight * gm[pl.ds(8 + EDGE - k, count)]
            front = front + weight * gm[pl.ds(8 - k, 8)]
        low[:, at] = total.astype(BF16)
        tail[:, at] = total[count - 16 :]
        edge[:, at] = front
        small_ref[G_STATE : G_STATE + EDGE, at] = is_first * front[:EDGE]
        small_ref[G_STATE + EDGE :, at] = jnp.zeros((16 - G_STATE - EDGE, BLOCK), F32)
        return carry

    for x, j in ((3, 1), (3, 2)):
        gg[:, :, x, 16 * j : 16 * j + 16, :] = jnp.zeros((4, 4, 16, BLOCK), BF16)
    loop(0, blocks, grads_step, 1)
    edge_copy = push(edge, edge_in, edge_sem.at[0], edge_sem.at[1], behind)
    edge_copy.start()
    save(gg, gg_hbm)
    core = lax.axis_index("mp")
    result_half[...] = (hidden_ref[...] + sums.total()).astype(BF16)
    result_ref[core] = result_half[...]
    result_copy = push(result_half, result_ref.at[core], core_sem.at[0], core_sem.at[1], other)
    result_copy.start()
    edge_copy.wait_recv()
    last = jnp.concatenate([tail[0:13], tail[13:16] + has_next * edge_in[0:EDGE]], axis=0)
    low[count - 16 :] = last.astype(BF16)
    result_copy.wait()
    for copy in saves:
        copy.wait()
    sums.drain()
    prefix.drain()
    edge_copy.wait_send()


def rec_back(
    gh, branch, normed, gate_lin, states_ext, factors, vectors, hidden,
    w_back, ext, mixed, reset, gated, gates, w_gate, mlp_part, cid,
):
    count, rec = gate_lin.shape
    half, width = hidden.shape

    def like(array):
        return pltpu.VMEM(array.shape, array.dtype)

    wide, low = pltpu.VMEM((count, rec), F32), pltpu.VMEM((count, rec), BF16)
    cube, gate_cube = (4, 4, 4, width // 64, rec), (4, 4, 4, GATE_ROWS, BLOCK)
    return pl.pallas_call(
        rec_back_kernel,
        out_shape=[
            jax.ShapeDtypeStruct((16, rec), F32),
            jax.ShapeDtypeStruct((2, half, width), F32),
            jax.ShapeDtypeStruct((count, rec), BF16),
            jax.ShapeDtypeStruct((2, half, width), BF16),
            jax.ShapeDtypeStruct(cube, BF16),
            jax.ShapeDtypeStruct(cube, BF16),
            jax.ShapeDtypeStruct(gate_cube, BF16),
        ],
        in_specs=[VM] * 8 + [ANY] * 8,
        out_specs=[VM] * 4 + [HBM] * 3,
        scratch_shapes=[
            like(w_back), like(ext), like(mixed), like(reset), like(gated), like(gates), like(w_gate), like(mlp_part),
            low, wide, wide, pltpu.VMEM((count + 16, BLOCK), F32),
            pltpu.VMEM(cube, BF16), pltpu.VMEM(cube, BF16), pltpu.VMEM(gate_cube, BF16),
            pltpu.VMEM((16, rec), F32), pltpu.VMEM((8, rec), F32), pltpu.VMEM((8, rec), F32),
            pltpu.VMEM((3, 4, 2, rec), F32), pltpu.VMEM((half, width), BF16),
            DMA((8,)),
            DMA((3,)),
            DMA((1, 3, 3)),
            DMA((1, 3, 3)),
            DMA((2,)),
            DMA((2,)),
        ]
        + ring_sum_scratch(half, width),
        compiler_params=params(cid, 61),
    )(
        gh, branch, normed, gate_lin, states_ext, factors, vectors, hidden,
        w_back, ext, mixed, reset, gated, gates, w_gate, mlp_part,
    )


def rec_end_kernel(
    part_in_ref, small_ref, gain_term_ref, gh_ref, tokens_in, inverse_ref, gain_ref, normed_ref, low_ref,
    dw0, dw1, gg_hbm, wl_hbm,
    total_ref, gains_ref, all_gates_ref, out0, out1, out2, tokens_hbm,
    *refs,
):
    bufs, refs = refs[: 78 + 3 * 6], refs[78 + 3 * 6 :]
    (
        part, dw2, wl, gates_out, part_low, part_in, tokens_v, gates_ref, ring_gains, gains0, small0, small1, small2,
        load_sem, own_sem, send, recv, gsend, grecv, small_send, small_recv, ring_send, ring_recv, core_sem,
    ) = refs
    half, width = gh_ref.shape
    load = pltpu.make_async_copy(wl_hbm, wl, load_sem.at[0])
    load.start()
    core = lax.axis_index("mp")
    other = {"mp": 1 - core}
    x_here = lax.axis_index("x")
    greet(axis_peers() + [other] + [{"x": peer, "mp": 1 - core} for peer in ring("x")[1:]])
    small = [
        Total(slots, small_send, small_recv, e, ORDERS[e])
        for e, slots in enumerate((small0, small1, small2))
    ]
    for flow, (start, wide) in zip(small, CHUNKS):
        flow.start(small_ref[:, start : start + wide])
    gates = [
        Scatter(
            9 + e, gg_hbm, (0, BLOCK), ORDERS[e], None, bufs[78 + 6 * e : 84 + 6 * e], gates_out,
            own_sem, send, recv, BANDS[e],
        )
        for e in range(3)
    ]
    flows = [
        Scatter(
            e, (dw0, dw1, dw2)[e // 3], CHUNKS[e % 3], SUM_ORDERS[e // 3][e % 3], ROW_HALVES,
            bufs[9 * e : 9 * e + 9] if e < 6 else bufs[8 * e + 6 : 8 * e + 14], (out0, out1, out2)[e // 3],
            own_sem, send, recv, rings=2 if e < 6 else 1,
        )
        for e in range(9)
    ]
    one, two, three = flows[:3], flows[3:6], flows[6:]
    spread = [Gather(e, gates_ref, ORDERS[e], (0, BLOCK), gsend, grecv, band=BANDS[e]) for e in range(3)]

    def each(group, name, *args):
        for flow in group:
            getattr(flow, name)(*args)

    each(gates, "begin", 0)
    each(one, "begin", 0)
    each(two, "begin", 0)

    def weight_grad(i, carry):
        cols = pl.ds(pl.multiple_of(i * 256, 256), 256)
        shard_rows(dw2, i, outer(normed_ref[:, cols], low_ref[...]).astype(BF16))
        return carry

    lax.fori_loop(0, width // 256, weight_grad, 0)
    each(three, "begin", 0)
    each(gates, "finish")
    each(gates, "begin", 1)
    for flow in small:
        flow.step()
    load.wait()

    def part_tile(i, carry):
        at = pl.ds(pl.multiple_of(i * 256, 256), 256)
        value = dot_t(low_ref[...], wl[at, :])
        part[0, :, at] = part_in_ref[0, :, at] + value[:half]
        part[1, :, at] = part_in_ref[1, :, at] + value[half:]
        return carry

    lax.fori_loop(0, width // 256, part_tile, 0)
    part_low[...] = part[1 - core].astype(BF16)
    part_copy = push(part_low, part_in, core_sem.at[0], core_sem.at[1], other)
    part_copy.start()
    each(one, "middle")
    part_copy.wait_recv()
    grad_normed = part[core] + part_in[...].astype(F32)
    mine = pl.ds(pl.multiple_of(core * half, half), half)
    inverse = inverse_ref[mine]
    hat = tokens_in[mine].astype(F32) * inverse
    gain_term = jnp.sum(grad_normed * hat, axis=0, keepdims=True)
    quarter = width // 4
    for k in range(4):
        cols = slice(k * quarter, (k + 1) * quarter)
        ring_gains[x_here, core, k : k + 1] = gain_term[:, cols]
        ring_gains[x_here, core, 4 + k : 5 + k] = gain_term_ref[:, cols]
    shares = []
    spot = ring_gains.at[x_here, core]
    group = [{"x": x, "mp": c} for x in ring("x") for c in (core, 1 - core)][1:]
    for k, peer in enumerate(group):
        copy = push(spot, spot, ring_send.at[k], ring_recv.at[k], peer)
        copy.start()
        shares.append(copy)
    grad_hat = grad_normed * gain_ref[...]
    inner = jnp.mean(grad_hat * hat, axis=-1, keepdims=True)
    tokens_v[...] = gh_ref[...] + inverse * (grad_hat - hat * inner)
    token_copy = push(tokens_v, tokens_hbm.at[core], core_sem.at[2], core_sem.at[3], other)
    token_copy.start()
    token_save = pltpu.make_async_copy(tokens_v, tokens_hbm.at[core], load_sem.at[1])
    token_save.start()
    each(two, "middle")
    each(gates, "finish")
    each(gates, "begin", 2)
    for flow in small:
        flow.step()
    each(one, "finish")
    each(one, "begin", 1)
    for copy in shares:
        copy.wait_recv()
    gains = Total(gains0, small_send, small_recv, 3, ("y", "z"))
    halves = [ring_gains[x, 0] + ring_gains[x, 1] for x in range(4)]
    gains.start((halves[0] + halves[1]) + (halves[2] + halves[3]))
    each(three, "middle")
    each(gates, "finish")
    gates_ref[lax.axis_index("z"), lax.axis_index("y"), x_here] = gates_out[...].astype(BF16)
    each(spread, "begin", 0)
    for flow, (start, wide) in zip(small, CHUNKS):
        total_ref[:, start : start + wide] = flow.step()
    each(two, "finish")
    each(two, "begin", 1)
    gains.step()
    each(one, "middle")
    each(spread, "finish")
    each(spread, "begin", 1)
    each(three, "finish")
    each(three, "begin", 1)
    each(two, "middle")
    each(one, "finish")
    each(one, "begin", 2)
    gains_ref[...] = gains.step()
    each(spread, "finish")
    each(spread, "begin", 2)
    each(two, "finish")
    each(two, "begin", 2)
    each(one, "finish")
    each(three, "finish")
    each(three, "begin", 2)
    each(two, "finish")
    each(spread, "finish")

    def unpack(b, carry):
        at = pl.ds(pl.multiple_of(16 * lax.rem(b, 3), 16), 16)
        all_gates_ref[b] = gates_ref[:, :, b // 3, at, :].reshape(BLOCK, BLOCK).astype(F32)
        return carry

    lax.fori_loop(0, all_gates_ref.shape[0], unpack, 0)
    each(three, "finish")
    for copy in (token_copy, token_save):
        copy.wait()
    each(flows + gates + spread + small, "drain")
    gains.drain()
    for copy in shares + [part_copy]:
        copy.wait_send()


def rec_end(part, small, gain_term, grad_hidden, tokens, inverse, gain, normed, low, weights, gates, w_lin, cid):
    half, width = grad_hidden.shape
    rows, rec = weights[0].shape[3:]
    gate_blocks = 2 * rec // BLOCK

    def sds(*shape):
        return jax.ShapeDtypeStruct(shape, F32)

    bufs = []
    for e in range(9):
        bufs += scatter_buffers(rows, CHUNKS[e % 3][1], 2 if e < 6 else 1)
    for _ in range(3):
        bufs += scatter_buffers(GATE_ROWS // 3, BLOCK, 0)
    return pl.pallas_call(
        rec_end_kernel,
        out_shape=[
            sds(16, rec),
            sds(8, width // 4),
            sds(gate_blocks, BLOCK, BLOCK),
            sds(rows, rec),
            sds(rows, rec),
            sds(rows, rec),
            sds(2, half, width),
        ],
        in_specs=[VM] * 9 + [ANY] * 4,
        out_specs=[VM] * 6 + [HBM],
        scratch_shapes=bufs
        + [
            pltpu.VMEM(part.shape, F32),
            pltpu.VMEM(weights[0].shape, BF16),
            pltpu.VMEM(w_lin.shape, BF16),
            pltpu.VMEM((GATE_ROWS, BLOCK), F32),
            pltpu.VMEM((half, width), BF16),
            pltpu.VMEM((half, width), BF16),
            pltpu.VMEM((half, width), F32),
            pltpu.VMEM(gates.shape, BF16),
            pltpu.VMEM((4, 2, 8, width // 4), F32),
            pltpu.VMEM((2, 4, 8, width // 4), F32),
        ]
        + [pltpu.VMEM((3, 4, 16, wide), F32) for _, wide in CHUNKS]
        + [
            DMA((2,)),
            DMA((12, 3)),
            DMA((12, 3, 3, 3)),
            DMA((12, 3, 3, 3)),
            DMA((3, 3, 1, 3)),
            DMA((3, 3, 1, 3)),
            DMA((4, 3, 3)),
            DMA((4, 3, 3)),
            DMA((7,)),
            DMA((7,)),
            DMA((4,)),
        ],
        compiler_params=params(cid, 60),
    )(part, small, gain_term, grad_hidden, tokens, inverse, gain, normed, low, *weights, gates, w_lin)


def mlp_end_kernel(in_ref, back, send, recv):
    x_here = lax.axis_index("x")
    peers = ring("x")[1:]
    greet([{"x": peer} for peer in peers])
    moves = []
    for step, peer in enumerate(peers):
        copy = push(in_ref.at[peer], back.at[x_here], send.at[step], recv.at[step], {"x": peer})
        copy.start()
        moves.append(copy)
    back[x_here] = in_ref[x_here]
    for copy in moves:
        copy.wait()


def mlp_end(quarters, cid):
    return pl.pallas_call(
        mlp_end_kernel,
        out_shape=jax.ShapeDtypeStruct(quarters.shape, quarters.dtype),
        in_specs=[VM],
        out_specs=VM,
        scratch_shapes=[DMA((3,)), DMA((3,))],
        compiler_params=params(cid, 61),
    )(quarters)


def finish_kernel(
    small_hbm, gains_hbm, out_hbm, gate_hbm, lin_hbm, back_hbm, rms_hbm, rms_mlp_hbm, result_in, tokens_in, gates_in,
    result_ref, tokens_ref, gates_ref, rec_ref, out_ref, mlp_ref, down_ref, bias_ref, lam_ref, conv_w_ref, conv_b_ref,
    gain_rec_ref, gain_mlp_ref, h_ref, state_ref, rms_ref, rms_mlp_ref,
    small_ref, gains_ref, out_sums, gate_sums, lin_sums, back, rms_v, rms_mlp_v, result_v, tokens_v, gates_v, sem, out_sem,
):
    pairs = (
        (result_in, result_v), (tokens_in, tokens_v), (gates_in, gates_v),
        (small_hbm, small_ref), (gains_hbm, gains_ref), (out_hbm, out_sums), (gate_hbm, gate_sums),
        (lin_hbm, lin_sums), (back_hbm, back), (rms_hbm, rms_v), (rms_mlp_hbm, rms_mlp_v),
    )
    loads = [pltpu.make_async_copy(src, dst, sem.at[k]) for k, (src, dst) in enumerate(pairs)]
    for load in loads:
        load.start()
    copies = []
    for k, (src, dst) in enumerate(((result_v, result_ref), (tokens_v, tokens_ref), (gates_v, gates_ref))):
        loads[k].wait()
        copies.append(pltpu.make_async_copy(src, dst, out_sem.at[k]))
        copies[k].start()
    for load in loads[3:]:
        load.wait()
    rec_ref[:, 0, :] = gate_sums[...]
    rec_ref[:, 1, :] = lin_sums[...]
    out_ref[...] = out_sums[...]
    units = down_ref.shape[1] // 4
    for q in range(4):
        value = back[q].astype(F32)
        at = pl.ds(q * units, units)
        for k in range(2):
            mlp_ref[:, k, at] = value[:, k * units : (k + 1) * units]
        down_ref[:, at] = value[:, 2 * units :]
    bias_ref[...] = small_ref[G_BIAS : G_BIAS + 2]
    lam_ref[...] = small_ref[G_LAM]
    conv_w_ref[...] = small_ref[G_CONV_W : G_CONV_W + CONV]
    conv_b_ref[...] = small_ref[G_CONV_B]
    h_ref[...] = small_ref[G_H]
    state_ref[...] = small_ref[G_STATE : G_STATE + EDGE]
    quarter = gains_ref.shape[1]
    for k in range(4):
        at = pl.ds(k * quarter, quarter)
        gain_rec_ref[at] = gains_ref[k]
        gain_mlp_ref[at] = gains_ref[4 + k]
    half = rms_mlp_v.shape[1]
    square = (half, half)
    diagonal = lax.broadcasted_iota(jnp.int32, square, 0) == lax.broadcasted_iota(jnp.int32, square, 1)
    for core in range(2):
        at = pl.ds(core * half, half)
        for ref, column in ((rms_ref, rms_v[at, 0:1]), (rms_mlp_ref, rms_mlp_v[core, :, 0:1])):
            spread = jnp.where(diagonal, jnp.broadcast_to(column, square), 0.0)
            ref[at] = jnp.sum(spread, axis=0)
    for copy in copies:
        copy.wait()


def finish(small, gains, sums, back, rms, rms_mlp, result, tokens, gates):
    rec = small.shape[1]
    rows = back.shape[1]
    units = back.shape[2] // 3
    width = gains.size // 2

    def sds(*shape):
        return jax.ShapeDtypeStruct(shape, F32)

    return pl.pallas_call(
        finish_kernel,
        out_shape=[
            jax.ShapeDtypeStruct(result.shape, result.dtype),
            sds(*tokens.shape),
            sds(*gates.shape),
            sds(rows, 2, rec),
            sds(rows, rec),
            sds(rows, 2, 4 * units),
            sds(rows, 4 * units),
            sds(2, rec),
            sds(rec),
            sds(CONV, rec),
            sds(rec),
            sds(width),
            sds(width),
            sds(rec),
            sds(EDGE, rec),
            sds(rms.shape[0]),
            sds(rms.shape[0]),
        ],
        in_specs=[HBM] * 11,
        out_specs=[HBM] * 3 + [VM] * 14,
        scratch_shapes=[pltpu.VMEM(a.shape, a.dtype) for a in (small, gains, *sums, back, rms, rms_mlp, result, tokens, gates)]
        + [DMA((11,)), DMA((3,))],
        compiler_params=pltpu.CompilerParams(vmem_limit_bytes=61 * MIB),
    )(small, gains, *sums, back, rms, rms_mlp, result, tokens, gates)


def body(
    tokens,
    cotangent,
    starts,
    valid,
    w_rec,
    w_out,
    w_mlp,
    w_down,
    lru_gates,
    lru_bias,
    lam,
    conv_w,
    conv_b,
    gain_rec,
    gain_mlp,
    h_init,
    conv_state,
):
    count, width = tokens.shape
    shard, _, rec = w_rec.shape
    hidden_units = w_mlp.shape[2] // 4
    half = count // 2
    core = lax.axis_index("mp")

    (
        w_lin, w_gate, w_back, mlp_weights, ext, gate_lin, mixed, reset, gated, factors, states_ext, branch_in,
        normed_rec, grad_out_all, inverse_rec, rms_rec, hidden, normed_mlp, inverse_mlp, rms_half, grad_out, vectors,
    ) = rec_forward(
        tokens,
        gain_rec,
        gain_mlp,
        (conv_w, conv_b, lam, lru_bias, conv_state, h_init),
        (starts, valid),
        w_rec,
        w_out.T,
        w_mlp,
        w_down.T,
        cotangent,
        lru_gates,
        0,
    )
    w_lin, w_gate, w_back = (w.reshape(width, rec) for w in (w_lin, w_gate, w_back))
    grad_hidden, grad_hidden_low, gain_mlp_term, mlp_terms, mlp_part = mlp(
        normed_mlp, grad_out, hidden, inverse_mlp, gain_mlp[None], grad_out_all, mlp_weights, 1
    )
    mlp_sums = lax.psum_scatter(mlp_terms, ("z", "y"), scatter_dimension=0, tiled=True)
    grad_hidden_low = grad_hidden_low.reshape(count, width)
    small, normed_part, grad_rec_low, result, *weight_terms, gate_terms = rec_back(
        grad_hidden_low,
        branch_in,
        normed_rec,
        gate_lin,
        states_ext,
        factors,
        vectors,
        hidden,
        w_back,
        ext,
        mixed,
        reset,
        gated,
        lru_gates,
        w_gate,
        mlp_part,
        2,
    )
    small, gains, gate_blocks, out_sums, gate_sums, lin_sums, grad_tokens = rec_end(
        normed_part,
        small,
        gain_mlp_term,
        grad_hidden,
        tokens,
        inverse_rec,
        gain_rec[None],
        normed_rec,
        grad_rec_low,
        weight_terms,
        gate_terms,
        w_lin,
        3,
    )
    back = mlp_end(mlp_sums.reshape(4, shard, 3 * hidden_units), 4)
    (
        result, grad_tokens, grad_gates, grad_w_rec, grad_out_t, grad_w_mlp, grad_down_t, grad_bias, grad_lam,
        grad_conv_w, conv_bias_gradient, grad_gain_rec, grad_gain_mlp, grad_h_init, grad_conv_state, rms_rec, rms_mlp,
    ) = finish(
        small,
        gains,
        (out_sums, gate_sums, lin_sums),
        back,
        rms_rec,
        rms_half,
        result.reshape(count, width),
        grad_tokens.reshape(count, width),
        gate_blocks.reshape(lru_gates.shape),
    )
    return (
        result,
        rms_rec,
        rms_mlp,
        grad_tokens,
        grad_w_rec,
        grad_out_t.T,
        grad_w_mlp,
        grad_down_t.T,
        grad_gates,
        grad_bias,
        grad_lam,
        grad_conv_w,
        conv_bias_gradient,
        grad_gain_rec,
        grad_gain_mlp,
        grad_h_init,
        grad_conv_state,
    )


def solution(mesh):
    cube = Mesh(mesh.devices.reshape(4, 4, 4, 2), ("z", "y", "x", "mp"))
    placed = (
        P(SEQ, None),
        P(SEQ, None),
        P(SEQ),
        P(SEQ),
        P(SEQ, None, "mp"),
        P("mp", SEQ),
        P(SEQ, None, "mp"),
        P("mp", SEQ),
        P(None, "mp", None, None),
        P(None, "mp"),
        P("mp"),
        P(None, "mp"),
        P("mp"),
        P(),
        P(),
        P("mp"),
        P(None, "mp"),
    )
    return jax.shard_map(
        body,
        mesh=cube,
        in_specs=placed,
        out_specs=(
            P(SEQ, None),
            P(SEQ),
            P(SEQ),
            P(SEQ, None),
            P(SEQ, None, "mp"),
            P("mp", SEQ),
            P(SEQ, None, "mp"),
            P("mp", SEQ),
            P(None, "mp", None, None),
            P(None, "mp"),
            P("mp"),
            P(None, "mp"),
            P("mp"),
            P(),
            P(),
            P("mp"),
            P(None, "mp"),
        ),
        check_vma=False,
    )
```

profile of v0, /device:TPU:0, one launch (start us, length us, event | category | flops | bytes accessed | tf_op | source)
XLA Modules:
  0.0 373.5 jit_solution(6968166259107386459)
XLA Ops:
  7.2 0.0 reduce-scatter.2.cloned.1.call-start
  7.2 118.4 %shard_map.296 = (bf16[4,4,4,32,1280]{4,3,2,1,0:T(8,128)(2,1)}, bf16[4,4,4,32,1280]{4,3,2,1,0:T(8,128)(2,1)}, bf16[4,4,4,32,1280]{4,3,2,1,0:T(8,128)(2,1)}, bf16...) custom-call(bf16[256,2048]{1,0:T(8,128)(2,1)} %tokens_in.1, ...), custom_call_target="tpu_custom_call" | custom-call | tf_op jit(solution)/shard_map/pallas_call | solution.py:996
  125.7 70.5 %shard_map.297 = (f32[128,2048]{1,0:T(8,128)}, bf16[2,128,2048]{2,1,0:T(8,128)(2,1)}, f32[1,2048]{1,0:T(1,128)}, bf16[2048,2304]{1,0:T(8,128)(2,1)}, bf16[4,2,128,2048]{3,2,1,0:T(8,128)(2,1)}) custom-call(bf16[128,2048]{1,0:T(8,128)(2,1)} %get-tuple-element.75.nm_ref, bf16[128,2048]{1,0:T(8,128)(2,1)} %get-tuple-element.76.go_ref, ...), custom_call_target="tpu_custom_call" | custom-call | tf_op jit(solution)/shard_map/pallas_call | solution.py:627
  196.2 0.0 reduce-scatter.2.cloned.1.call-update
  196.2 44.2 %shard_map.298 = (f32[16,1280]{1,0:T(8,128)}, f32[2,128,2048]{2,1,0:T(8,128)}, bf16[256,1280]{1,0:T(8,128)(2,1)}, bf16[2,128,2048]{2,1,0:T(8,128)(2,1)}, bf16[4,...) custom-call(bf16[256,2048]{1,0:T(8,128)(2,1)} %bitcast.22, ...), custom_call_target="tpu_custom_call" | custom-call | tf_op jit(solution)/shard_map/pallas_call | solution.py:1210
  240.4 108.2 %shard_map.299 = (f32[16,1280]{1,0:T(8,128)}, f32[8,512]{1,0:T(8,128)}, f32[10,256,256]{2,1,0:T(8,128)}, f32[32,1280]{1,0:T(8,128)}, f32[32,1280]{1,0:T(8,128)},...) custom-call(f32[2,128,2048]{2,1,0:T(8,128)} %get-tuple-element.95.part_in_ref, f32[16,1280]{1,0:T(8,128)} %get-tuple-element.96.small_ref, ...), custom_call_target="tpu_custom_call" | custom-call | tf_op jit(solution)/shard_map/pallas_call | solution.py:1412
  348.7 0.0 reduce-scatter.2.cloned.1.call-done
  348.7 11.7 %shard_map.300.back_hbm = bf16[4,32,2304]{2,1,0:T(8,128)(2,1)} custom-call(bf16[4,32,2304]{2,1,0:T(8,128)(2,1)} %bitcast.23), custom_call_target="tpu_custom_call" | custom-call | tf_op jit(solution)/shard_map/pallas_call | solution.py:1471
  360.4 6.3 %shard_map.301 = (bf16[256,2048]{1,0:T(8,128)(2,1)}, f32[256,2048]{1,0:T(8,128)}, f32[2,5,256,256]{3,2,1,0:T(8,128)}, f32[32,2,1280]{2,1,0:T(2,128)}, f32[32,128...) custom-call(f32[16,1280]{1,0:T(8,128)} %get-tuple-element.105.small_, ...), custom_call_target="tpu_custom_call" | custom-call | tf_op jit(solution)/shard_map/pallas_call | solution.py:1544
Async XLA Ops:
  7.2 341.5 %reduce-scatter.2.cloned.1.call-start = ((), (), s32[]{:S(2)}) async-start(), calls=%async_computation.1 | async-start | bytes 10027008 | tf_op jit(solution)/shard_map/reduce_scatter | solution.py:1619
Sparse Core Ops, SparseCore 0:
  196.3 103.1 reduce-scatter.1
where the time goes:
time: 374 us
  Pallas kernels  359 us (96%)
  between operations  14.1 us (4%)
    pallas_call x1, Pallas kernels, rec_forward(): pl.pallas_call(rec_forward_kernel, out_shape=[sds(*one) for one in saved...  118 us
    pallas_call x1, Pallas kernels, rec_end(): pl.pallas_call(rec_end_kernel, out_shape=[sds(16, rec), sds(8, width // 4...  108 us
    pallas_call x1, Pallas kernels, mlp(): pl.pallas_call(mlp_kernel, out_shape=[jax.ShapeDtypeStruct((rows, width),...  70.5 us
    pallas_call x1, Pallas kernels, rec_back(): pl.pallas_call(rec_back_kernel, out_shape=[jax.ShapeDtypeStruct((16, rec)...  44.2 us
    pallas_call x1, Pallas kernels, mlp_end(): pl.pallas_call(mlp_end_kernel, out_shape=jax.ShapeDtypeStruct(quarters.sh...  11.7 us
  transfers between devices with their start and end apart: 1, of which 0 were waited for; matrix products, arithmetic and copies ran while one was open for 0% of the time, Pallas kernels for 41%

commit v1 on v0

--- a/solution.py
+++ b/solution.py
@@ -583,7 +583,7 @@
             dw_ref[tile(i), pl.ds(2 * units, units)] = outer(go[:, tile(i)], mlp_in[...]).astype(BF16)
             return carry
 
-        loop(lower, upper, step, 1)
+        loop(lower, upper, step, 2)
 
     sums = RingSum(npart, *sum_refs)
     for copy in across:
@@ -1453,7 +1453,7 @@
     )(part, small, gain_term, grad_hidden, tokens, inverse, gain, normed, low, *weights, gates, w_lin)
 
 
-def mlp_end_kernel(in_ref, back, send, recv):
+def mlp_end_kernel(in_ref, back, send, recv, own_sem):
     x_here = lax.axis_index("x")
     peers = ring("x")[1:]
     greet([{"x": peer} for peer in peers])
@@ -1462,18 +1462,20 @@
         copy = push(in_ref.at[peer], back.at[x_here], send.at[step], recv.at[step], {"x": peer})
         copy.start()
         moves.append(copy)
-    back[x_here] = in_ref[x_here]
+    own = pltpu.make_async_copy(in_ref.at[x_here], back.at[x_here], own_sem)
+    own.start()
     for copy in moves:
         copy.wait()
+    own.wait()
 
 
 def mlp_end(quarters, cid):
     return pl.pallas_call(
         mlp_end_kernel,
         out_shape=jax.ShapeDtypeStruct(quarters.shape, quarters.dtype),
-        in_specs=[VM],
+        in_specs=[HBM],
         out_specs=VM,
-        scratch_shapes=[DMA((3,)), DMA((3,))],
+        scratch_shapes=[DMA((3,)), DMA((3,)), DMA],
         compiler_params=params(cid, 61),
     )(quarters)
 

time: 374 us -> 372 us (level)
  no operation moved by 1% of the time
where the time goes in v1:
time: 372 us
  Pallas kernels  358 us (96%)
  between operations  14.1 us (4%)
    pallas_call x1, Pallas kernels, rec_forward(): pl.pallas_call(rec_forward_kernel, out_shape=[sds(*one) for one in saved...  118 us
    pallas_call x1, Pallas kernels, rec_end(): pl.pallas_call(rec_end_kernel, out_shape=[sds(16, rec), sds(8, width // 4...  108 us
    pallas_call x1, Pallas kernels, mlp(): pl.pallas_call(mlp_kernel, out_shape=[jax.ShapeDtypeStruct((rows, width),...  69.3 us
    pallas_call x1, Pallas kernels, rec_back(): pl.pallas_call(rec_back_kernel, out_shape=[jax.ShapeDtypeStruct((16, rec)...  44.8 us
    pallas_call x1, Pallas kernels, mlp_end(): pl.pallas_call(mlp_end_kernel, out_shape=jax.ShapeDtypeStruct(quarters.sh...  10.9 us
  transfers between devices with their start and end apart: 1, of which 0 were waited for; matrix products, arithmetic and copies ran while one was open for 0% of the time, Pallas kernels for 41%

profile of v1, /device:TPU:0, one launch (start us, length us, event | category | flops | bytes accessed | tf_op | source)
XLA Modules:
  0.0 371.7 jit_solution(11541795785581824407)
XLA Ops:
  7.2 0.0 reduce-scatter.2.cloned.1.call-start
  7.2 118.4 %shard_map.296 = (bf16[4,4,4,32,1280]{4,3,2,1,0:T(8,128)(2,1)}, bf16[4,4,4,32,1280]{4,3,2,1,0:T(8,128)(2,1)}, bf16[4,4,4,32,1280]{4,3,2,1,0:T(8,128)(2,1)}, bf16...) custom-call(bf16[256,2048]{1,0:T(8,128)(2,1)} %tokens_in.1, ...), custom_call_target="tpu_custom_call" | custom-call | tf_op jit(solution)/shard_map/pallas_call | solution.py:996
  125.7 69.3 %shard_map.297 = (f32[128,2048]{1,0:T(8,128)}, bf16[2,128,2048]{2,1,0:T(8,128)(2,1)}, f32[1,2048]{1,0:T(1,128)}, bf16[2048,2304]{1,0:T(8,128)(2,1)}, bf16[4,2,128,2048]{3,2,1,0:T(8,128)(2,1)}) custom-call(bf16[128,2048]{1,0:T(8,128)(2,1)} %get-tuple-element.75.nm_ref, bf16[128,2048]{1,0:T(8,128)(2,1)} %get-tuple-element.76.go_ref, ...), custom_call_target="tpu_custom_call" | custom-call | tf_op jit(solution)/shard_map/pallas_call | solution.py:627
  195.0 0.0 reduce-scatter.2.cloned.1.call-update
  195.0 44.8 %shard_map.298 = (f32[16,1280]{1,0:T(8,128)}, f32[2,128,2048]{2,1,0:T(8,128)}, bf16[256,1280]{1,0:T(8,128)(2,1)}, bf16[2,128,2048]{2,1,0:T(8,128)(2,1)}, bf16[4,...) custom-call(bf16[256,2048]{1,0:T(8,128)(2,1)} %bitcast.22, ...), custom_call_target="tpu_custom_call" | custom-call | tf_op jit(solution)/shard_map/pallas_call | solution.py:1210
  239.7 107.9 %shard_map.299 = (f32[16,1280]{1,0:T(8,128)}, f32[8,512]{1,0:T(8,128)}, f32[10,256,256]{2,1,0:T(8,128)}, f32[32,1280]{1,0:T(8,128)}, f32[32,1280]{1,0:T(8,128)},...) custom-call(f32[2,128,2048]{2,1,0:T(8,128)} %get-tuple-element.95.part_in_ref, f32[16,1280]{1,0:T(8,128)} %get-tuple-element.96.small_ref, ...), custom_call_target="tpu_custom_call" | custom-call | tf_op jit(solution)/shard_map/pallas_call | solution.py:1412
  347.6 0.0 reduce-scatter.2.cloned.1.call-done
  347.7 10.9 %shard_map.300.back_hbm = bf16[4,32,2304]{2,1,0:T(8,128)(2,1)} custom-call(bf16[4,32,2304]{2,1,0:T(8,128)(2,1)} %bitcast.23), custom_call_target="tpu_custom_call" | custom-call | tf_op jit(solution)/shard_map/pallas_call | solution.py:1473
  358.6 6.3 %shard_map.301 = (bf16[256,2048]{1,0:T(8,128)(2,1)}, f32[256,2048]{1,0:T(8,128)}, f32[2,5,256,256]{3,2,1,0:T(8,128)}, f32[32,2,1280]{2,1,0:T(2,128)}, f32[32,128...) custom-call(f32[16,1280]{1,0:T(8,128)} %get-tuple-element.105.small_, ...), custom_call_target="tpu_custom_call" | custom-call | tf_op jit(solution)/shard_map/pallas_call | solution.py:1546
Async XLA Ops:
  7.2 340.5 %reduce-scatter.2.cloned.1.call-start = ((), (), s32[]{:S(2)}) async-start(), calls=%async_computation.1 | async-start | bytes 10027008 | tf_op jit(solution)/shard_map/reduce_scatter | solution.py:1621
Sparse Core Ops, SparseCore 0:
  195.1 103.4 reduce-scatter.1

commit v2 on v1

--- a/solution.py
+++ b/solution.py
@@ -365,9 +365,9 @@
 
 CHUNKS = ((0, 384), (384, 512), (896, 384))
 SUM_ORDERS = (
-    (("y", "z", "x"), ("x", "y", "z"), ("z", "y", "x")),
-    (("z", "x", "y"), ("x", "z", "y"), ("y", "x", "z")),
     (("y", "z", "x"), ("x", "y", "z"), ("z", "x", "y")),
+    (("x", "z", "y"), ("z", "x", "y"), ("y", "z", "x")),
+    (("y", "x", "z"), ("x", "y", "z"), ("z", "y", "x")),
 )
 ROW_HALVES = (pl.ds(0, 16), pl.ds(16, 16))
 BANDS = ((0, 16), (16, 16), (32, 16))

time: 372 us -> 376 us (1.011)
  Pallas kernels: 358 us -> 362 us
  transfers between devices with their start and end apart: 1 -> 1, of which waited for: 0 -> 0; matrix products, arithmetic and copies ran while one was open for 0% -> 0% of each run, Pallas kernels for 41% -> 42%
where the time goes in v2:
time: 376 us
  Pallas kernels  362 us (96%)
  between operations  14.1 us (4%)
    pallas_call x1, Pallas kernels, rec_forward(): pl.pallas_call(rec_forward_kernel, out_shape=[sds(*one) for one in saved...  118 us
    pallas_call x1, Pallas kernels, rec_end(): pl.pallas_call(rec_end_kernel, out_shape=[sds(16, rec), sds(8, width // 4...  111 us
    pallas_call x1, Pallas kernels, mlp(): pl.pallas_call(mlp_kernel, out_shape=[jax.ShapeDtypeStruct((rows, width),...  69.3 us
    pallas_call x1, Pallas kernels, rec_back(): pl.pallas_call(rec_back_kernel, out_shape=[jax.ShapeDtypeStruct((16, rec)...  44.8 us
    pallas_call x1, Pallas kernels, mlp_end(): pl.pallas_call(mlp_end_kernel, out_shape=jax.ShapeDtypeStruct(quarters.sh...  11.6 us
  transfers between devices with their start and end apart: 1, of which 0 were waited for; matrix products, arithmetic and copies ran while one was open for 0% of the time, Pallas kernels for 42%

profile of v2, /device:TPU:0, one launch (start us, length us, event | category | flops | bytes accessed | tf_op | source)
XLA Modules:
  0.0 375.9 jit_solution(13114209027069867080)
XLA Ops:
  7.2 0.0 reduce-scatter.2.cloned.1.call-start
  7.2 118.4 %shard_map.296 = (bf16[4,4,4,32,1280]{4,3,2,1,0:T(8,128)(2,1)}, bf16[4,4,4,32,1280]{4,3,2,1,0:T(8,128)(2,1)}, bf16[4,4,4,32,1280]{4,3,2,1,0:T(8,128)(2,1)}, bf16...) custom-call(bf16[256,2048]{1,0:T(8,128)(2,1)} %tokens_in.1, ...), custom_call_target="tpu_custom_call" | custom-call | tf_op jit(solution)/shard_map/pallas_call | solution.py:996
  125.7 69.3 %shard_map.297 = (f32[128,2048]{1,0:T(8,128)}, bf16[2,128,2048]{2,1,0:T(8,128)(2,1)}, f32[1,2048]{1,0:T(1,128)}, bf16[2048,2304]{1,0:T(8,128)(2,1)}, bf16[4,2,128,2048]{3,2,1,0:T(8,128)(2,1)}) custom-call(bf16[128,2048]{1,0:T(8,128)(2,1)} %get-tuple-element.75.nm_ref, bf16[128,2048]{1,0:T(8,128)(2,1)} %get-tuple-element.76.go_ref, ...), custom_call_target="tpu_custom_call" | custom-call | tf_op jit(solution)/shard_map/pallas_call | solution.py:627
  195.0 0.0 reduce-scatter.2.cloned.1.call-update
  195.0 44.8 %shard_map.298 = (f32[16,1280]{1,0:T(8,128)}, f32[2,128,2048]{2,1,0:T(8,128)}, bf16[256,1280]{1,0:T(8,128)(2,1)}, bf16[2,128,2048]{2,1,0:T(8,128)(2,1)}, bf16[4,...) custom-call(bf16[256,2048]{1,0:T(8,128)(2,1)} %bitcast.22, ...), custom_call_target="tpu_custom_call" | custom-call | tf_op jit(solution)/shard_map/pallas_call | solution.py:1210
  239.7 111.4 %shard_map.299 = (f32[16,1280]{1,0:T(8,128)}, f32[8,512]{1,0:T(8,128)}, f32[10,256,256]{2,1,0:T(8,128)}, f32[32,1280]{1,0:T(8,128)}, f32[32,1280]{1,0:T(8,128)},...) custom-call(f32[2,128,2048]{2,1,0:T(8,128)} %get-tuple-element.95.part_in_ref, f32[16,1280]{1,0:T(8,128)} %get-tuple-element.96.small_ref, ...), custom_call_target="tpu_custom_call" | custom-call | tf_op jit(solution)/shard_map/pallas_call | solution.py:1412
  351.2 0.0 reduce-scatter.2.cloned.1.call-done
  351.2 11.6 %shard_map.300.back_hbm = bf16[4,32,2304]{2,1,0:T(8,128)(2,1)} custom-call(bf16[4,32,2304]{2,1,0:T(8,128)(2,1)} %bitcast.23), custom_call_target="tpu_custom_call" | custom-call | tf_op jit(solution)/shard_map/pallas_call | solution.py:1473
  362.8 6.3 %shard_map.301 = (bf16[256,2048]{1,0:T(8,128)(2,1)}, f32[256,2048]{1,0:T(8,128)}, f32[2,5,256,256]{3,2,1,0:T(8,128)}, f32[32,2,1280]{2,1,0:T(2,128)}, f32[32,128...) custom-call(f32[16,1280]{1,0:T(8,128)} %get-tuple-element.105.small_, ...), custom_call_target="tpu_custom_call" | custom-call | tf_op jit(solution)/shard_map/pallas_call | solution.py:1546
Async XLA Ops:
  7.2 344.0 %reduce-scatter.2.cloned.1.call-start = ((), (), s32[]{:S(2)}) async-start(), calls=%async_computation.1 | async-start | bytes 10027008 | tf_op jit(solution)/shard_map/reduce_scatter | solution.py:1621
Sparse Core Ops, SparseCore 0:
  195.1 103.2 reduce-scatter.1
